TPU v7x, 512 devices: a whole 4x4x16 slice. The times are simulated.
512 devices in a mesh: rep: 16 (over x_hi, y, core), tp: 32 (over x_lo, z).
Axes of the slice: x: 4 (x_hi: 2, x_lo: 2; x = x_hi * 2 + x_lo), y: 4, z: 16, core: 2. Of those that a mesh axis runs over, the one named last changes fastest.
Arguments:
- hidden_old: bfloat16 [2, 1024, 8192], P(None, 'rep', 'tp'), parts along dimension 1, may hold values from -6 to 6
- queries_old: bfloat16 [16384, 8, 128], P(('rep', 'tp')), parts along dimension 0, may hold values from -25 to 25
- kv_weight: bfloat16 [8192, 4096], P(None, 'tp'), may hold values from -0.0625 to 0.0625
- cache: bfloat16 [16384, 64, 256], P(('rep', 'tp')), parts along dimension 0, may hold values from -6 to 6
- lengths: int32 [1024], P('rep'), parts along dimension 0, may hold values from 2 to 63, as said below
- slot: int32 [1024], P('rep'), parts along dimension 0, may hold values from 0 to 63, as said below
- hidden_new: bfloat16 [2, 1024, 8192], P(None, 'rep', 'tp'), parts along dimension 1, may hold values from -6 to 6
- queries_new: bfloat16 [1024, 128, 128], P(('rep', 'tp')), parts along dimension 0, may hold values from -25 to 25
Outputs:
- attended_old: bfloat16 [16384, 8, 128], P(('rep', 'tp')), parts along dimension 0
- attended_new: bfloat16 [1024, 128, 128], P(('rep', 'tp')), parts along dimension 0
- served: bfloat16 [1024, 1024, 256], P(('rep', 'tp')), parts along dimension 0
There are 16 independent parts, one for each index of `rep`. A program takes and returns all parts, laid end to end along the dimension named above; an argument that names none is the same for every part. Nothing has to cross between parts.
Inputs may be any that keep to these rules, and one draw needn't show every extreme that they name: `lengths`: in every draw one sequence has 63 filled positions and another has 2. `slot`: a permutation in which sequences r < 32 take even positions and the others odd positions.
All inputs are finite; a program needn't handle non-finite values.
Results may differ from a plain program's by a relative error of at most 0.0065.
Values may be sent and summed in bfloat16 or wider, within the bound.
A program may use at most 64 MiB of HBM per device.

v0:
```python
import jax
import jax.numpy as jnp
from jax import lax
from jax.sharding import PartitionSpec as P


def swapped(block, axis, bit):
    count = lax.axis_size(axis)
    route = []
    for low in range(count):
        high = low | 1 << bit
        if high != low and high < count:
            route += [(low, high), (high, low)]
    return lax.ppermute(block, axis, route)


def attend(queries, key_rows, value_rows, own_keys, own_values, valid_mask):
    score_scale = 1.0 / queries.shape[-1] ** 0.5
    scores = (
        jnp.einsum("abge,able->abgl", queries, key_rows, preferred_element_type=jnp.float32)
        * score_scale
    )
    own_score = (
        jnp.einsum("abge,abe->abg", queries, own_keys, preferred_element_type=jnp.float32)
        * score_scale
    )
    scores = jnp.where(valid_mask[:, :, None, :], scores, -jnp.inf)
    row_max = jnp.maximum(jnp.max(scores, axis=-1), own_score)
    weights = jnp.exp(scores - row_max[..., None])
    own_weight = jnp.exp(own_score - row_max)
    row_total = jnp.sum(weights, axis=-1) + own_weight
    weights = (weights / row_total[..., None]).astype(jnp.bfloat16)
    own_weight = (own_weight / row_total).astype(jnp.bfloat16)
    attended = jnp.einsum(
        "abgl,able->abge", weights, value_rows, preferred_element_type=jnp.float32
    )
    attended = (
        attended
        + own_weight.astype(jnp.float32)[..., None] * own_values.astype(jnp.float32)[:, :, None, :]
    )
    return attended.astype(jnp.bfloat16)


def regroup(received, share_rows, part_count):
    trailing = received.shape[2:]
    heads_all = received.shape[1] // part_count
    grouped = received.reshape((share_rows // part_count, heads_all, part_count) + trailing)
    grouped = jnp.swapaxes(grouped, 1, 2)
    return grouped.reshape((share_rows, heads_all) + trailing)


def shards(hidden_old, queries_old, kv_weight, cache, lengths, slot, hidden_new, queries_new):
    members = lax.axis_size("tp")
    my_index = lax.axis_index("tp")
    row_count = lengths.shape[0]
    entry_count, span_len, pair_cols = cache.shape
    group_size = queries_old.shape[1]
    head_dim = queries_old.shape[2]
    heads_here = max(1, entry_count // row_count)
    rows_here = entry_count // heads_here
    part_count = row_count // rows_here
    my_part = my_index % part_count
    first_row = my_part * rows_here
    share_rows = row_count // members
    section_no = my_index // (members // 2)
    gathered = lax.all_gather(hidden_old, "tp", axis=2, tiled=True)
    inputs = lax.dynamic_index_in_dim(gathered, section_no, 0, keepdims=False)
    fresh_cols = jnp.dot(inputs, kv_weight, preferred_element_type=jnp.float32).astype(jnp.bfloat16)
    own_rows = lax.dynamic_slice_in_dim(fresh_cols, first_row, rows_here, 0)
    foreign_rows = lax.dynamic_slice_in_dim(fresh_cols, (1 - my_part) * rows_here, rows_here, 0)
    partner = swapped(foreign_rows, "tp", 0)
    keys_part = jnp.where(my_part == 0, own_rows, partner)
    values_part = jnp.where(my_part == 0, partner, own_rows)
    fresh_here = jnp.concatenate([keys_part, values_part], axis=1)[None]
    stored = cache.reshape(heads_here, rows_here, span_len, pair_cols)
    my_len = lax.dynamic_slice_in_dim(lengths, first_row, rows_here)
    position = lax.broadcasted_iota(jnp.int32, (rows_here, span_len), 1)
    valid_old = (position < my_len[:, None])[None]
    old_out = attend(
        queries_old.reshape(heads_here, rows_here, group_size, head_dim),
        stored[..., :head_dim],
        stored[..., head_dim:],
        fresh_here[..., :head_dim],
        fresh_here[..., head_dim:],
        valid_old,
    )
    attended_old = old_out.reshape(entry_count, group_size, head_dim)
    order_rows = (
        jnp.zeros((row_count,), jnp.int32).at[slot].set(jnp.arange(row_count, dtype=jnp.int32))
    )
    order_pairs = order_rows.reshape(row_count // part_count, part_count)
    local_order = lax.dynamic_index_in_dim(order_pairs, my_part, 1, keepdims=False) - first_row
    served_len = jnp.take(lengths, order_rows) + 1
    my_len_new = lax.dynamic_slice_in_dim(served_len, my_index * share_rows, share_rows)
    new_pos = lax.broadcasted_iota(jnp.int32, (share_rows, span_len), 1)
    landing = (position == my_len[:, None])[None, :, :, None]
    appended = jnp.where(landing, fresh_here[:, :, None, :], stored)
    sending = jnp.swapaxes(jnp.take(appended, local_order, axis=1), 0, 1)
    served_here = regroup(
        lax.all_to_all(sending, "tp", split_axis=0, concat_axis=1, tiled=True),
        share_rows,
        part_count,
    )
    weight_rows = lax.all_to_all(kv_weight, "tp", split_axis=0, concat_axis=1, tiled=True)
    feature_count = weight_rows.shape[0]
    layer_cols = weight_rows.shape[1] // 2
    weight_layers = weight_rows.reshape(feature_count, 2, layer_cols)
    product = jnp.einsum(
        "lrd,dlc->rlc", hidden_new, weight_layers, preferred_element_type=jnp.float32
    )
    fresh_new = lax.psum_scatter(
        product.reshape(lax.axis_size("tp") * share_rows, 2 * layer_cols),
        "tp",
        scatter_dimension=0,
        tiled=True,
    ).astype(jnp.bfloat16)
    heads_all = served_here.shape[1]
    new_pairs = fresh_new.reshape(share_rows, heads_all, pair_cols)
    valid_new = (new_pos < my_len_new[:, None])[:, None, :]
    new_out = attend(
        queries_new.reshape(share_rows, heads_all, group_size, head_dim),
        served_here[..., :head_dim],
        served_here[..., head_dim:],
        new_pairs[..., :head_dim],
        new_pairs[..., head_dim:],
        valid_new,
    )
    attended_new = new_out.reshape(share_rows, heads_all * group_size, head_dim)
    served = served_here.reshape(share_rows, heads_all * span_len, pair_cols)
    return (attended_old, attended_new, served)


def solution(mesh):
    placed = (
        P(None, "rep", "tp"),
        P(("rep", "tp"), None, None),
        P(None, "tp"),
        P(("rep", "tp"), None, None),
        P("rep"),
        P("rep"),
        P(None, "rep", "tp"),
        P(("rep", "tp"), None, None),
    )
    return jax.shard_map(
        shards,
        mesh=mesh,
        in_specs=placed,
        out_specs=(
            P(("rep", "tp"), None, None),
            P(("rep", "tp"), None, None),
            P(("rep", "tp"), None, None),
        ),
        check_vma=False,
    )
```

profile of v0, /device:TPU:24, one launch (start us, length us, event | category | flops | bytes accessed | tf_op | source)
XLA Modules:
  0.0 382.9 jit_solution(11594560024683008989)
XLA Ops:
  7.2 16.7 %all-to-all-start.1 = ((bf16[32,256,128]{2,1,0:T(8,128)(2,1)}), bf16[32,256,128]{2,1,0:T(8,128)(2,1)}, u32[]{:S(2)}, u32[]{:S(2)}) async-start(bf16[32,256,128]{2,1,0:T(8,128)(2,1)} %bitcast.66), calls=%async_computation.1 | async-start | bytes 4194304 | tf_op jit(solution)/shard_map/all_to_all | solution.py:104
  24.0 0.7 all-gather.2.cloned.1.call-update
  24.7 0.8 scatter_custom_fusion
  25.5 0.1 reshape.184
  25.6 0.1 dynamic_slice.20
  25.7 0.2 fusion.22
  25.9 0.1 iota_compare_fusion
  26.0 174.1 %all-gather.2.cloned.1.call-done = bf16[2,64,8192]{2,1,0:T(8,128)(2,1)} async-done(((bf16[2,64,256]{2,1,0:T(8,128)(2,1)}), bf16[2,64,8192]{2,1,0:T(8,128)(2,1)}) %all-gather.2.cloned.1.call-update) | async-done | bytes 2097168 | tf_op jit(solution)/shard_map/all_gather | solution.py:66
  200.1 1.7 convolution_convert_fusion
  201.8 2.2 collective-permute-start
  204.1 0.8 gather_fusion
  204.9 1.3 dynamic-slice
  206.8 0.2 and_reduce_fusion
  207.0 2.2 collective-permute-done
  209.2 0.4 broadcast_select_fusion
  209.7 0.6 gather_fusion.1
  210.3 1.1 bitcast_select_fusion
  211.4 7.0 %all-to-all-start = ((bf16[32,1,64,256]{3,2,1,0:T(8,128)(2,1)}), bf16[32,1,64,256]{3,2,1,0:T(8,128)(2,1)S(1)}, u32[]{:S(2)}, u32[]{:S(2)}) async-start(bf16[32,1,64,256]{3,2,1,0:T(8,128)(2,1)} %bitcast_select_fusion), calls=%async_computation | async-start | bytes 2097152 | tf_op jit(solution)/shard_map/all_to_all | solution.py:100
  218.5 0.1 dynamic_slice.24
  218.6 0.1 iota_compare_fusion.2
  218.6 0.5 fusion.34
  219.1 0.2 fusion.20
  219.3 0.2 fusion.10
  219.5 1.0 fusion.3
  220.5 3.3 copy.19
  223.7 0.7 convolution_bitcast_fusion
  224.5 0.1 copy.27
  224.6 149.5 %all-reduce.2 = bf16[64,4096]{1,0:T(8,128)(2,1)S(1)} all-reduce(f32[64,4096]{1,0:T(8,128)S(1)} %bitcast.69), channel_id=2, replica_groups=mesh['rep'=16,'tp'=32] {'tp'}, use_global_device_ids=true, to_apply=%region_4.5.clone | all-reduce | flops 262144 | bytes 1572864
  374.1 0.1 fusion.12
  374.4 0.5 fusion.35
  374.8 0.2 fusion.11
  375.1 1.0 fusion.5
  (39 shorter events, 0.3 us)
Async XLA Ops:
  7.2 216.6 %copy-start = (bf16[2,64,256]{2,1,0:T(8,128)(2,1)S(1)}, bf16[2,64,256]{2,1,0:T(8,128)(2,1)}, u32[]{:S(2)}) copy-start(bf16[2,64,256]{2,1,0:T(8,128)(2,1)} %param.14) | copy-start | bytes 196612
  7.2 17.5 %copy-start.8 = (s32[64]{0:T(128)S(1)}, s32[64]{0:T(128)}, u32[]{:S(2)}) copy-start(s32[64]{0:T(128)} %param.13) | copy-start | bytes 772
  7.2 18.4 %copy-start.1 = (s32[64]{0:T(128)S(1)}, s32[64]{0:T(128)}, u32[]{:S(2)}) copy-start(s32[64]{0:T(128)} %param.12) | copy-start | bytes 772
  7.2 192.9 %copy-start.2 = (bf16[8192,128]{1,0:T(8,128)(2,1)S(1)}, bf16[8192,128]{1,0:T(8,128)(2,1)}, u32[]{:S(2)}) copy-start(bf16[8192,128]{1,0:T(8,128)(2,1)} %param.10) | copy-start | bytes 6291460
  7.2 204.2 %all-to-all-start.1 = ((bf16[32,256,128]{2,1,0:T(8,128)(2,1)}), bf16[32,256,128]{2,1,0:T(8,128)(2,1)}, u32[]{:S(2)}, u32[]{:S(2)}) async-start(bf16[32,256,128]{2,1,0:T(8,128)(2,1)} %bitcast.66), calls=%async_computation.1 | async-start | bytes 4194304 | tf_op jit(solution)/shard_map/all_to_all | solution.py:104
  23.9 185.3 %copy-start.3 = (bf16[32,64,256]{2,1,0:T(8,128)(2,1)S(1)}, bf16[32,64,256]{2,1,0:T(8,128)(2,1)}, u32[]{:S(2)}) copy-start(bf16[32,64,256]{2,1,0:T(8,128)(2,1)} %param.11) | copy-start | bytes 3145732
  23.9 176.2 %all-gather.2.cloned.1.call-start = ((), (), s32[]{:S(2)}) async-start(), calls=%async_computation.2 | async-start | bytes 2162688 | tf_op jit(solution)/shard_map/all_gather | solution.py:66
  201.8 7.3 %collective-permute-start = (bf16[32,128]{1,0:T(8,128)(2,1)S(1)}, bf16[32,128]{1,0:T(8,128)(2,1)S(1)}, u32[]{:S(2)}, u32[]{:S(2)}) collective-permute-start(bf16[32,128]{1,0:T(8,128)(2,1)S(1)} %constant_dynamic-slice_fusion), channel_id=1, source_target_pairs={{0,1},{1,0},{2,3},{3,2},{4,5},{5,4},{6,7},{7,6},{8,9},{9,8},{10,11... | collective-permute-start | bytes 24584 | tf_op jit(solution)/shard_map/ppermute | solution.py:14
  210.3 8.4 %copy-start.4 = (bf16[32,64,256]{2,1,0:T(8,128)(2,1)S(1)}, bf16[32,64,256]{2,1,0:T(8,128)(2,1)}, u32[]{:S(2)}) copy-start(bf16[32,64,256]{2,1,0:T(8,128)(2,1)} %param.11) | copy-start | bytes 3145732
  210.3 8.3 %copy-start.6 = (bf16[32,8,128]{2,1,0:T(8,128)(2,1)S(1)}, bf16[32,8,128]{2,1,0:T(8,128)(2,1)}, u32[]{:S(2)}) copy-start(bf16[32,8,128]{2,1,0:T(8,128)(2,1)} %param.9) | copy-start | bytes 196612
  211.4 162.8 %all-to-all-start = ((bf16[32,1,64,256]{3,2,1,0:T(8,128)(2,1)}), bf16[32,1,64,256]{3,2,1,0:T(8,128)(2,1)S(1)}, u32[]{:S(2)}, u32[]{:S(2)}) async-start(bf16[32,1,64,256]{3,2,1,0:T(8,128)(2,1)} %bitcast_select_fusion), calls=%async_computation | async-start | bytes 2097152 | tf_op jit(solution)/shard_map/all_to_all | solution.py:100
  224.5 149.6 %copy-start.7 = (bf16[2,128,128]{2,1,0:T(8,128)(2,1)S(1)}, bf16[2,128,128]{2,1,0:T(8,128)(2,1)}, u32[]{:S(2)}) copy-start(bf16[2,128,128]{2,1,0:T(8,128)(2,1)} %param.15) | copy-start | bytes 196612
  374.4 1.7 copy-start.5
Sparse Core Ops, SparseCore 0:
  26.8 173.2 all-gather.1
where the time goes:
time: 385 us; the launch traced here: 383 us
  waiting for transfers between devices  177 us (46%)
  blocking collectives  149 us (39%)
  starting transfers between devices  25.9 us (7%)
  between operations  15.1 us (4%)
  local copies, waits for them, and re-layouts  7.19 us (2%)
  matrix products  5.6 us (1%)
    all_gather x1, waiting for transfers between devices, shards(): gathered = lax.all_gather(hidden_old, 'tp', axis=2, tiled=True)  174 us
    unnamed x1, blocking collectives  149 us
    all_to_all x1, starting transfers between devices, shards(): lax.all_to_all(kv_weight, 'tp', split_axis=0, concat_axis=1, tiled=True)  16.7 us
  transfers between devices with their start and end apart: 4, of which 2 were waited for; matrix products, arithmetic and copies ran while one was open for 4% of the time, Pallas kernels for 0%

commit v1 on v0

v1 whole, which is shorter than its diff:
```python
import jax
import jax.numpy as jnp
from jax import lax
from jax.experimental import pallas as pl
from jax.experimental.pallas import tpu as pltpu
from jax.sharding import PartitionSpec as P

MESH = pl.DeviceIdType.MESH
TP = 32
NZ = 16


def remote(src, dst, send_sem, recv_sem, target):
    return pltpu.make_async_remote_copy(
        src_ref=src,
        dst_ref=dst,
        send_sem=send_sem,
        recv_sem=recv_sem,
        device_id={"tp": target},
        device_id_type=MESH,
    )


def exchange_kernel(
    order_ref,
    key_ref,
    hold_ref,
    hnew_ref,
    w_hbm,
    cache_hbm,
    raw_ref,
    fresh_ref,
    pair_ref,
    hbuf,
    wbuf,
    cbuf,
    sbuf,
    mbuf,
    obuf,
    acc,
    local_sem,
    xs_sem,
    xr_sem,
    gs_sem,
    gr_sem,
    cs_sem,
    cr_sem,
    ms_sem,
    mr_sem,
    ps_sem,
    pr_sem,
):
    me = lax.axis_index("tp")
    x = me // NZ
    z = me % NZ
    other = 1 - x
    half = z % 2
    head = me // 2

    load_own = [
        pltpu.make_async_copy(hold_ref.at[x], hbuf.at[z, x, pl.ds(0, 64)], local_sem.at[0]),
        pltpu.make_async_copy(hnew_ref.at[x], hbuf.at[z, x, pl.ds(64, 64)], local_sem.at[1]),
    ]
    load_w = pltpu.make_async_copy(w_hbm, wbuf, local_sem.at[2])
    load_c = pltpu.make_async_copy(cache_hbm, cbuf, local_sem.at[3])
    for c in load_own:
        c.start()
    load_c.start()
    load_w.start()

    barrier = pltpu.get_barrier_semaphore()
    for d in range(1, TP):
        pl.semaphore_signal(barrier, inc=1, device_id={"tp": (me + d) % TP}, device_id_type=MESH)
    pl.semaphore_wait(barrier, TP - 1)

    twin = other * NZ + z
    xcopies = [
        remote(hold_ref.at[other], hbuf.at[z, x, pl.ds(0, 64)], xs_sem.at[0], xr_sem.at[0], twin),
        remote(hnew_ref.at[other], hbuf.at[z, x, pl.ds(64, 64)], xs_sem.at[1], xr_sem.at[1], twin),
    ]
    for c in xcopies:
        c.start()

    right = x * NZ + (z + 1) % NZ
    left = x * NZ + (z + NZ - 1) % NZ
    steps = ((8, 7), (7, 8))
    planes = (x, other)
    sent = []

    def ring(stream, way, k):
        slot = (z + (NZ - k if way == 0 else k)) % NZ
        block = hbuf.at[slot, planes[stream]]
        where = (stream * 2 + way) * 8 + k
        return remote(block, block, gs_sem.at[where], gr_sem.at[where], right if way == 0 else left)

    def multiply(stream, slot):
        plane = planes[stream]
        rows = pl.ds(pl.multiple_of((plane * NZ + slot) * 256, 256), 256)
        acc[...] += jnp.dot(
            hbuf[slot, plane], wbuf[rows, :], preferred_element_type=jnp.float32
        )

    offsets = []
    for dz in (8, 7, 9, 6, 10, 5, 11, 4, 12, 3, 13, 2, 14, 1, 15, 0):
        for dx in (0, 1):
            if dz or dx:
                offsets.append((dx, dz))
    cache_copies = []

    def send_block(j):
        dx, dz = offsets[j]
        target = (x + dx) % 2 * NZ + (z + dz) % NZ
        sbuf[j] = cbuf[order_ref[target]]
        c = remote(sbuf.at[j], raw_ref.at[half, head], cs_sem.at[j], cr_sem.at[j], target)
        c.start()
        cache_copies.append(c)

    acc[...] = jnp.zeros_like(acc)
    for c in load_own:
        c.wait()
    for way in range(2):
        c = ring(0, way, 0)
        c.start()
        sent.append(c)
    for c in xcopies:
        c.wait_recv()
    for way in range(2):
        c = ring(1, way, 0)
        c.start()
        sent.append(c)
    load_c.wait()
    for j in range(4):
        send_block(j)
    load_w.wait()
    multiply(0, z)
    multiply(1, z)
    done = 4
    for k in range(8):
        for stream in range(2):
            for way in range(2):
                if k >= steps[stream][way]:
                    continue
                ring(stream, way, k).wait_recv()
                if k + 1 < steps[stream][way]:
                    c = ring(stream, way, k + 1)
                    c.start()
                    sent.append(c)
                multiply(stream, (z + (NZ - k - 1 if way == 0 else k + 1)) % NZ)
        for j in range(done, min(done + 4, len(offsets))):
            send_block(j)
        done = min(done + 4, len(offsets))

    fresh = acc[...].astype(jnp.bfloat16)
    rid = lax.broadcasted_iota(jnp.int32, (TP * 16, 128), 0)
    j = rid & 15
    d = rid >> 4
    wanted = jnp.where(j < 2, 2 * d + j, jnp.where(j < 4, 62 + 2 * d + j, -1))
    pick = (key_ref[...] == wanted).astype(jnp.bfloat16)
    messages = jnp.dot(pick, fresh, preferred_element_type=jnp.float32).astype(jnp.bfloat16)
    mbuf[...] = messages.reshape(TP, 16, 128)
    obuf[...] = fresh[:64].reshape(2, 32, 128)
    partner = x * NZ + z + 1 - 2 * half
    pcopy = remote(obuf.at[1 - half], pair_ref.at[half], ps_sem, pr_sem, partner)
    pcopy.start()
    message_copies = []
    for i in range(1, TP):
        target = (me + i) % TP
        c = remote(mbuf.at[target], fresh_ref.at[me], ms_sem.at[i], mr_sem.at[i], target)
        c.start()
        message_copies.append(c)
    pair_ref[half] = obuf[half]
    fresh_ref[me] = mbuf[me]
    sbuf[TP - 1] = cbuf[order_ref[me]]
    mine = pltpu.make_async_copy(sbuf.at[TP - 1], raw_ref.at[half, head], local_sem.at[4])
    mine.start()

    for c in sent:
        c.wait_send()
    for c in xcopies:
        c.wait_send()
    pcopy.wait()
    for c in message_copies:
        c.wait()
    for c in cache_copies:
        c.wait()
    mine.wait()


def exchange(order, key, hidden_old, hidden_new, kv_weight, cache):
    any_spec = pl.BlockSpec(memory_space=pl.ANY)
    vmem = pl.BlockSpec(memory_space=pltpu.VMEM)
    smem = pl.BlockSpec(memory_space=pltpu.SMEM)
    dma = pltpu.SemaphoreType.DMA
    bf = jnp.bfloat16
    return pl.pallas_call(
        exchange_kernel,
        out_shape=(
            jax.ShapeDtypeStruct((2, 16, 64, 256), bf),
            jax.ShapeDtypeStruct((TP, 16, 128), bf),
            jax.ShapeDtypeStruct((2, 32, 128), bf),
        ),
        in_specs=[smem, vmem, any_spec, any_spec, any_spec, any_spec],
        out_specs=(any_spec, vmem, vmem),
        scratch_shapes=[
            pltpu.VMEM((NZ, 2, 128, 256), bf),
            pltpu.VMEM((8192, 128), bf),
            pltpu.VMEM((32, 64, 256), bf),
            pltpu.VMEM((32, 64, 256), bf),
            pltpu.VMEM((TP, 16, 128), bf),
            pltpu.VMEM((2, 32, 128), bf),
            pltpu.VMEM((128, 128), jnp.float32),
            dma((5,)),
            dma((2,)),
            dma((2,)),
            dma((32,)),
            dma((32,)),
            dma((31,)),
            dma((31,)),
            dma((32,)),
            dma((32,)),
            dma,
            dma,
        ],
        compiler_params=pltpu.CompilerParams(
            collective_id=0, has_side_effects=True, vmem_limit_bytes=24 * 1024 * 1024
        ),
        cost_estimate=pl.CostEstimate(
            flops=2 * 128 * 8192 * 128, bytes_accessed=5 * 1024 * 1024, transcendentals=0
        ),
    )(order, key, hidden_old, hidden_new, kv_weight, cache)


def attend(queries, key_rows, value_rows, own_keys, own_values, valid_mask):
    score_scale = 1.0 / queries.shape[-1] ** 0.5
    scores = (
        jnp.einsum("abge,able->abgl", queries, key_rows, preferred_element_type=jnp.float32)
        * score_scale
    )
    own_score = (
        jnp.einsum("abge,abe->abg", queries, own_keys, preferred_element_type=jnp.float32)
        * score_scale
    )
    scores = jnp.where(valid_mask[:, :, None, :], scores, -jnp.inf)
    row_max = jnp.maximum(jnp.max(scores, axis=-1), own_score)
    weights = jnp.exp(scores - row_max[..., None])
    own_weight = jnp.exp(own_score - row_max)
    row_total = jnp.sum(weights, axis=-1) + own_weight
    weights = (weights / row_total[..., None]).astype(jnp.bfloat16)
    own_weight = (own_weight / row_total).astype(jnp.bfloat16)
    attended = jnp.einsum(
        "abgl,able->abge", weights, value_rows, preferred_element_type=jnp.float32
    )
    attended = (
        attended
        + own_weight.astype(jnp.float32)[..., None] * own_values.astype(jnp.float32)[:, :, None, :]
    )
    return attended.astype(jnp.bfloat16)


def shards(hidden_old, queries_old, kv_weight, cache, lengths, slot, hidden_new, queries_new):
    me = lax.axis_index("tp")
    half = me % 2
    first = half * 32
    my_slots = lax.dynamic_slice_in_dim(slot, first, 32)
    served_of = 2 * jnp.arange(TP, dtype=jnp.int32) + half
    hit = my_slots[None, :] == served_of[:, None]
    order = jnp.sum(jnp.where(hit, jnp.arange(32, dtype=jnp.int32)[None, :], 0), axis=1)
    key = jnp.concatenate([slot, jnp.arange(64, 128, dtype=jnp.int32)]).reshape(1, 128)
    raw, fresh, pair = exchange(order, key, hidden_old, hidden_new, kv_weight, cache)

    my_len = lax.dynamic_slice_in_dim(lengths, first, 32)
    position = lax.broadcasted_iota(jnp.int32, (32, 64), 1)
    valid_old = (position < my_len[:, None])[None]
    old_out = attend(
        queries_old[None],
        cache[None, ..., :128],
        cache[None, ..., 128:],
        pair[0][None],
        pair[1][None],
        valid_old,
    )
    attended_old = old_out.reshape(32, 8, 128)

    mine = 2 * me + jnp.arange(2, dtype=jnp.int32)
    new_len = jnp.sum(jnp.where(slot[None, :] == mine[:, None], lengths[None, :], 0), axis=1)
    landed = fresh[:, :4].reshape(16, 2, 2, 2, 128).transpose(2, 3, 0, 1, 4).reshape(2, 2, 16, 256)
    new_pos = lax.broadcasted_iota(jnp.int32, (2, 64), 1)
    landing = (new_pos == new_len[:, None])[:, None, :, None]
    served = jnp.where(landing, landed[0][:, :, None, :], raw)
    new_pairs = landed[1]
    valid_new = (new_pos < new_len[:, None] + 1)[:, None, :]
    new_out = attend(
        queries_new.reshape(2, 16, 8, 128),
        served[..., :128],
        served[..., 128:],
        new_pairs[..., :128],
        new_pairs[..., 128:],
        valid_new,
    )
    return (attended_old, new_out.reshape(2, 128, 128), served.reshape(2, 1024, 256))


def solution(mesh):
    placed = (
        P(None, "rep", "tp"),
        P(("rep", "tp"), None, None),
        P(None, "tp"),
        P(("rep", "tp"), None, None),
        P("rep"),
        P("rep"),
        P(None, "rep", "tp"),
        P(("rep", "tp"), None, None),
    )
    return jax.shard_map(
        shards,
        mesh=mesh,
        in_specs=placed,
        out_specs=(
            P(("rep", "tp"), None, None),
            P(("rep", "tp"), None, None),
            P(("rep", "tp"), None, None),
        ),
        check_vma=False,
    )
```

time: 385 us -> 110 us (0.29)
  waiting for transfers between devices: 177 us -> 0 us
  blocking collectives: 149 us -> 0 us
  Pallas kernels: 0 us -> 98.3 us
  starting transfers between devices: 25.9 us -> 0 us
  between operations: 15.1 us -> 0.83 us
    all_gather x1 -> x0, waiting for transfers between devices: 174 us -> none  [shards(): gathered = lax.all_gather(hidden_old, 'tp', axis=2, tiled=True)]
    unnamed x1 -> x0, blocking collectives: 149 us -> none
    pallas_call x0 -> x1, Pallas kernels: none -> 98.3 us  [exchange(): pl.pallas_call(exchange_kernel, out_shape=(jax.ShapeDtypeStruct((2, 16, 6...]
    all_to_all x2 -> x0, starting transfers between devices: 23.7 us -> none  [the longest x1 16.7 us: shards(): lax.all_to_all(kv_weight, 'tp', split_axis=0, concat_axis=1, tiled=True)]
  transfers between devices with their start and end apart: 4 -> 0, of which waited for: 2 -> 0; matrix products, arithmetic and copies ran while one was open for 4% -> 0% of each run, Pallas kernels for 0% -> 0%
where the time goes in v1:
time: 110 us
  Pallas kernels  98.3 us (89%)
  local copies, waits for them, and re-layouts  5.48 us (5%)
  matrix products  3.12 us (3%)
  other arithmetic  1.96 us (2%)
    pallas_call x1, Pallas kernels, exchange(): pl.pallas_call(exchange_kernel, out_shape=(jax.ShapeDtypeStruct((2, 16, 6...  98.3 us
    unnamed x20, local copies, waits for them, and re-layouts  4.53 us

profile of v1, /device:TPU:24, one launch (start us, length us, event | category | flops | bytes accessed | tf_op | source)
XLA Modules:
  0.0 109.7 jit_solution(6075957304397706772)
XLA Ops:
  0.6 0.0 copy-start
  0.6 0.0 copy-start.8
  0.7 0.0 copy-start.9
  0.7 0.8 dynamic_slice.7
  1.5 0.2 select_reduce_fusion.order_ref
  1.6 0.7 add_bitcast_fusion.key_ref
  2.4 1.2 %copy-done.1 = bf16[32,64,256]{2,1,0:T(8,128)(2,1)S(1)} copy-done((bf16[32,64,256]{2,1,0:T(8,128)(2,1)S(1)}, bf16[32,64,256]{2,1,0:T(8,128)(2,1)}, u32[]{:S(2)}) %copy-start.1) | copy-done | bytes 1048600
  3.6 1.6 %copy-done.3 = bf16[8192,128]{1,0:T(8,128)(2,1)S(1)} copy-done((bf16[8192,128]{1,0:T(8,128)(2,1)S(1)}, bf16[8192,128]{1,0:T(8,128)(2,1)}, u32[]{:S(2)}) %copy-start.3) | copy-done | bytes 2097176
  5.2 0.8 copy-done.4
  6.0 0.8 copy-done.5
  6.9 98.3 %shard_map.103 = (bf16[2,16,64,256]{3,2,1,0:T(8,128)(2,1)S(1)}, bf16[32,16,128]{2,1,0:T(8,128)(2,1)S(1)}, bf16[2,32,128]{2,1,0:T(8,128)(2,1)S(1)}) custom-call(s32[32]{0:T(128)S(1)} %select_reduce_fusion.order_ref, s32[1,128]{1,0:T(1,128)S(1)} %add_bitcast_fusion.key_ref, bf16[2,64,256]{2,1,0:T(8,128)(2,1)S(1)} %copy-done.4, ...), custom_call_target="tpu_custom_call" | custom-call | flops 268435456 | bytes 5242880 | tf_op jit(solution)/shard_map/pallas_call | solution.py:195
  105.3 0.0 copy-done.8
  105.3 0.0 copy-done.9
  105.3 0.2 fusion.26
  105.5 0.1 iota_compare_fusion.1
  105.6 0.2 broadcast_select_fusion
  105.8 0.0 copy-start.6
  105.8 0.1 iota_compare_fusion.2
  105.9 0.0 copy-done
  105.9 0.5 fusion.29
  106.4 0.1 fusion.12
  106.5 0.2 fusion.11
  106.8 1.0 fusion.5
  107.7 0.0 copy-done.7
  107.7 0.1 fusion.20
  107.9 0.1 dynamic_slice.6
  108.0 0.1 iota_compare_fusion
  108.0 0.0 copy-done.2
  108.0 0.5 fusion.28
  108.5 0.2 fusion.10
  108.7 1.0 fusion.3
  109.7 0.0 copy-done.6
  (21 shorter events, 0.2 us)
Async XLA Ops:
  0.6 105.2 %copy-start = (bf16[2,128,128]{2,1,0:T(8,128)(2,1)S(1)}, bf16[2,128,128]{2,1,0:T(8,128)(2,1)}, u32[]{:S(2)}) copy-start(bf16[2,128,128]{2,1,0:T(8,128)(2,1)} %param.15) | copy-start | bytes 196612
  0.6 104.7 %copy-start.8 = (s32[64]{0:T(128)S(1)}, s32[64]{0:T(128)}, u32[]{:S(2)}) copy-start(s32[64]{0:T(128)} %param.13) | copy-start | bytes 772
  0.7 104.7 %copy-start.9 = (s32[64]{0:T(128)S(1)}, s32[64]{0:T(128)}, u32[]{:S(2)}) copy-start(s32[64]{0:T(128)} %param.12) | copy-start | bytes 772
  2.4 1.2 %copy-start.1 = (bf16[32,64,256]{2,1,0:T(8,128)(2,1)S(1)}, bf16[32,64,256]{2,1,0:T(8,128)(2,1)}, u32[]{:S(2)}) copy-start(bf16[32,64,256]{2,1,0:T(8,128)(2,1)} %cache_hbm.1) | copy-start | bytes 3145732
  3.6 1.6 %copy-start.3 = (bf16[8192,128]{1,0:T(8,128)(2,1)S(1)}, bf16[8192,128]{1,0:T(8,128)(2,1)}, u32[]{:S(2)}) copy-start(bf16[8192,128]{1,0:T(8,128)(2,1)} %w_hbm.1) | copy-start | bytes 6291460
  5.2 0.8 copy-start.4
  6.0 0.8 copy-start.5
  105.6 2.1 %copy-start.7 = (bf16[32,8,128]{2,1,0:T(8,128)(2,1)S(1)}, bf16[32,8,128]{2,1,0:T(8,128)(2,1)}, u32[]{:S(2)}) copy-start(bf16[32,8,128]{2,1,0:T(8,128)(2,1)} %param.9) | copy-start | bytes 196612
  105.6 2.4 %copy-start.2 = (bf16[32,64,256]{2,1,0:T(8,128)(2,1)S(1)}, bf16[32,64,256]{2,1,0:T(8,128)(2,1)}, u32[]{:S(2)}) copy-start(bf16[32,64,256]{2,1,0:T(8,128)(2,1)} %cache_hbm.1) | copy-start | bytes 3145732
  105.8 3.9 %copy-start.6 = (bf16[2,16,64,256]{3,2,1,0:T(8,128)(2,1)}, bf16[2,16,64,256]{3,2,1,0:T(8,128)(2,1)S(1)}, u32[]{:S(2)}) copy-start(bf16[2,16,64,256]{3,2,1,0:T(8,128)(2,1)S(1)} %broadcast_select_fusion) | copy-start | bytes 3145732

commit v2 on v1

v2 whole, which is shorter than its diff:
```python
import jax
import jax.numpy as jnp
from jax import lax
from jax.experimental import pallas as pl
from jax.experimental.pallas import tpu as pltpu
from jax.sharding import PartitionSpec as P

MESH = pl.DeviceIdType.MESH
TP = 32
NZ = 16
SCALE = 1.0 / 128.0**0.5


def remote(src, dst, send_sem, recv_sem, target):
    return pltpu.make_async_remote_copy(
        src_ref=src,
        dst_ref=dst,
        send_sem=send_sem,
        recv_sem=recv_sem,
        device_id={"tp": target},
        device_id_type=MESH,
    )


def stored_part(queries, block, limit):
    keys = block[:, :, :128]
    values = block[:, :, 128:]
    scores = (
        jnp.einsum("egd,eld->egl", queries, keys, preferred_element_type=jnp.float32) * SCALE
    )
    position = lax.broadcasted_iota(jnp.int32, scores.shape, 2).astype(jnp.float32)
    scores = jnp.where(position < limit, scores, -jnp.inf)
    top = jnp.max(scores, axis=-1, keepdims=True)
    weights = jnp.exp(scores - top)
    total = jnp.sum(weights, axis=-1, keepdims=True)
    mixed = jnp.einsum(
        "egl,eld->egd", weights.astype(jnp.bfloat16), values, preferred_element_type=jnp.float32
    )
    return mixed, top, total


def with_tokens(queries, stored, tokens):
    mixed, top, total = stored
    query_f = queries.astype(jnp.float32)
    own = [jnp.sum(query_f * key, axis=-1, keepdims=True) * SCALE for key, _ in tokens]
    peak = top
    for score in own:
        peak = jnp.maximum(peak, score)
    shrink = jnp.exp(top - peak)
    mixed = mixed * shrink
    total = total * shrink
    for score, (_, value) in zip(own, tokens):
        weight = jnp.exp(score - peak)
        mixed = mixed + weight * value
        total = total + weight
    return mixed / total


def step_kernel(
    hold_hbm,
    qold_hbm,
    w_hbm,
    cache_hbm,
    len_hbm,
    slot_hbm,
    slot1_hbm,
    hnew_hbm,
    qnew_hbm,
    old_ref,
    new_ref,
    served_ref,
    hbuf,
    wbuf,
    cbuf,
    sbuf,
    mbuf,
    fbuf,
    obuf,
    pbuf,
    qobuf,
    qnbuf,
    len_row,
    slot_row,
    len_cols,
    pick_old,
    pick_new,
    acc,
    slot_s,
    order_s,
    local_sem,
    xs_sem,
    xr_sem,
    gs_sem,
    gr_sem,
    cs_sem,
    cr_sem,
    ms_sem,
    mr_sem,
    ps_sem,
    pr_sem,
    near_sem,
):
    me = lax.axis_index("tp")
    x = me // NZ
    z = me % NZ
    other = 1 - x
    half = z % 2
    head = me // 2

    def on_ring(dz):
        return x * NZ + (z + dz) % NZ

    right, left, twin = on_ring(1), on_ring(NZ - 1), other * NZ + z
    barrier = pltpu.get_barrier_semaphore()
    for peer in (right, left, twin):
        pl.semaphore_signal(barrier, inc=1, device_id={"tp": peer}, device_id_type=MESH)

    loads = [
        (slot1_hbm, slot_s),
        (hold_hbm.at[x], hbuf.at[z, x, 0]),
        (hnew_hbm.at[x], hbuf.at[z, x, 1]),
        (slot_hbm, slot_row),
        (len_hbm, len_row),
        (cache_hbm, cbuf),
        (w_hbm, wbuf),
        (qold_hbm, qobuf),
        (qnew_hbm, qnbuf),
    ]
    loads = [
        pltpu.make_async_copy(src, dst, local_sem.at[i]) for i, (src, dst) in enumerate(loads)
    ]
    for c in loads:
        c.start()
    loads[0].wait()

    def find(u, carry):
        found = 0
        for r in range(32):
            found = jnp.where(slot_s[32 * half + r] == 2 * u + half, r, found)
        order_s[u] = found
        return carry

    lax.fori_loop(0, TP, find, 0)
    for c in loads[1:5]:
        c.wait()

    pl.semaphore_wait(barrier, 3)

    xcopies = []
    for p, src in enumerate((hold_hbm, hnew_hbm)):
        c = remote(src.at[other], hbuf.at[z, x, p], xs_sem.at[p], xr_sem.at[p], twin)
        c.start()
        xcopies.append(c)

    steps = ((8, 7), (7, 8))
    planes = (x, other)
    sent = []

    def ring(stream, way, k, p):
        slot = (z + (NZ - k if way == 0 else k)) % NZ
        block = hbuf.at[slot, planes[stream], p]
        where = ((stream * 2 + way) * 8 + k) * 2 + p
        return remote(block, block, gs_sem.at[where], gr_sem.at[where], right if way == 0 else left)

    def forward(stream, way, k, p):
        c = ring(stream, way, k, p)
        c.start()
        sent.append(c)

    for p in range(2):
        for way in range(2):
            forward(0, way, 0, p)

    def greet(i, dist):
        for way, dz in ((0, dist), (1, NZ - dist)):
            pl.semaphore_signal(
                near_sem.at[2 * i + way],
                inc=1,
                device_id={"tp": on_ring(dz)},
                device_id_type=MESH,
            )

    def greeted(i):
        for way in range(2):
            pl.semaphore_wait(near_sem.at[2 * i + way], 1)

    greet(0, 1)
    for p in range(2):
        xcopies[p].wait_recv()
        for way in range(2):
            forward(1, way, 0, p)
    greeted(0)
    greet(1, 2)

    acc[...] = jnp.zeros_like(acc)
    rid = lax.broadcasted_iota(jnp.int32, (TP * 8, 64), 0)
    col = lax.broadcasted_iota(jnp.int32, (TP * 8, 64), 1)
    j = rid & 7
    d = rid >> 3
    pick_old[...] = (
        (slot_row[...] == jnp.where(j < 2, 2 * d + j, -1)).astype(jnp.float32).astype(jnp.bfloat16)
    )
    pick_new[...] = (
        (col == jnp.where((j >= 2) & (j < 4), 2 * d + j - 2, -1))
        .astype(jnp.float32)
        .astype(jnp.bfloat16)
    )
    eye = lax.broadcasted_iota(jnp.int32, (64, 64), 0) == lax.broadcasted_iota(
        jnp.int32, (64, 64), 1
    )
    lengths_f = len_row[...].astype(jnp.float32)
    column = jnp.sum(jnp.where(eye, lengths_f, 0.0), axis=1, keepdims=True)
    len_cols[...] = jnp.broadcast_to(column, (64, 128))

    greeted(1)
    greet(2, 4)
    loads[5].wait()
    greeted(2)

    order = [(0, 8)]
    for dz in range(7, 0, -1):
        order += [(0, dz), (1, dz), (0, NZ - dz), (1, NZ - dz)]
    order += [(1, 0), (1, 8)]
    cache_copies = []

    def send_blocks(count):
        for _ in range(count):
            i = len(cache_copies)
            if i == len(order):
                return
            dx, dz = order[i]
            target = (x + dx) % 2 * NZ + (z + dz) % NZ
            sbuf[i] = cbuf[order_s[target]]
            c = remote(
                sbuf.at[i], served_ref.at[half, head], cs_sem.at[i], cr_sem.at[i], target
            )
            c.start()
            cache_copies.append(c)

    def multiply(stream, slot):
        plane = planes[stream]
        rows = pl.ds(pl.multiple_of((plane * NZ + slot) * 256, 256), 256)
        acc[...] += jnp.dot(
            hbuf[slot, plane].reshape(128, 256), wbuf[rows, :], preferred_element_type=jnp.float32
        )

    send_blocks(5)
    loads[6].wait()
    for k in range(8):
        for stream in range(2):
            for p in range(2):
                for way in range(2):
                    if k >= steps[stream][way]:
                        continue
                    ring(stream, way, k, p).wait_recv()
                    if k + 1 < steps[stream][way]:
                        forward(stream, way, k + 1, p)
        send_blocks(4)
        if k == 0:
            multiply(0, z)
            multiply(1, z)
        for stream in range(2):
            for way in range(2):
                if k < steps[stream][way]:
                    multiply(stream, (z + (NZ - k - 1 if way == 0 else k + 1)) % NZ)

    fresh = acc[...].astype(jnp.bfloat16)
    obuf[...] = fresh[:64].reshape(2, 32, 128)
    partner = on_ring(NZ + 1 - 2 * half)
    pcopy = remote(obuf.at[1 - half], pbuf.at[half], ps_sem, pr_sem, partner)
    pcopy.start()
    messages = jnp.dot(pick_old[...], fresh[:64], preferred_element_type=jnp.float32) + jnp.dot(
        pick_new[...], fresh[64:], preferred_element_type=jnp.float32
    )
    mbuf[...] = messages.astype(jnp.bfloat16).reshape(TP, 8, 128)
    message_copies = []
    for i in range(1, TP):
        target = (me + i) % TP
        c = remote(mbuf.at[target], fbuf.at[me], ms_sem.at[i], mr_sem.at[i], target)
        c.start()
        message_copies.append(c)
    pbuf[half] = obuf[half]
    fbuf[me] = mbuf[me]
    served_ref[half, head] = cbuf[order_s[me]]

    loads[7].wait()
    loads[8].wait()
    stored_old = []
    for c in range(2):
        entries = pl.ds(16 * c, 16)
        limit = len_cols[pl.ds(pl.multiple_of(32 * half + 16 * c, 16), 16), :][:, None, :64]
        stored_old.append(stored_part(qobuf[entries], cbuf[entries], limit))
    pcopy.wait()
    for c in range(2):
        entries = pl.ds(16 * c, 16)
        tokens = [
            (
                pbuf[0, entries].astype(jnp.float32)[:, None, :],
                pbuf[1, entries].astype(jnp.float32)[:, None, :],
            )
        ]
        old_ref[entries] = with_tokens(qobuf[entries], stored_old[c], tokens).astype(jnp.bfloat16)

    for c in cache_copies:
        c.wait()
    stored_new = []
    new_len = []
    for p in range(2):
        count = jnp.sum(
            jnp.where(slot_row[...] == 2 * me + p, lengths_f, 0.0), axis=1, keepdims=True
        )
        new_len.append(count)
        queries = qnbuf[p].reshape(16, 8, 128)
        stored_new.append(stored_part(queries, served_ref[p], count.reshape(1, 1, 1)))
    for c in message_copies:
        c.wait()
    received = fbuf[...].astype(jnp.float32).reshape(16, 2, 8, 128)
    for p in range(2):
        queries = qnbuf[p].reshape(16, 8, 128)
        first_key, first_value = received[:, 0, p : p + 1], received[:, 1, p : p + 1]
        tokens = [
            (first_key, first_value),
            (received[:, 0, p + 2 : p + 3], received[:, 1, p + 2 : p + 3]),
        ]
        attended = with_tokens(queries, stored_new[p], tokens)
        new_ref[p] = attended.astype(jnp.bfloat16).reshape(128, 128)
        row = lax.broadcasted_iota(jnp.int32, (1, 64, 256), 1).astype(jnp.float32)
        token = jnp.concatenate([first_key, first_value], axis=2)
        served_ref[p] = jnp.where(
            row == new_len[p].reshape(1, 1, 1), token, served_ref[p].astype(jnp.float32)
        ).astype(jnp.bfloat16)

    for c in sent:
        c.wait_send()
    for c in xcopies:
        c.wait_send()


def shards(hidden_old, queries_old, kv_weight, cache, lengths, slot, hidden_new, queries_new):
    any_spec = pl.BlockSpec(memory_space=pl.ANY)
    vmem = pl.BlockSpec(memory_space=pltpu.VMEM)
    dma = pltpu.SemaphoreType.DMA
    bf = jnp.bfloat16
    attended_old, attended_new, served = pl.pallas_call(
        step_kernel,
        out_shape=(
            jax.ShapeDtypeStruct((32, 8, 128), bf),
            jax.ShapeDtypeStruct((2, 128, 128), bf),
            jax.ShapeDtypeStruct((2, 16, 64, 256), bf),
        ),
        in_specs=[any_spec] * 9,
        out_specs=(vmem, vmem, vmem),
        scratch_shapes=[
            pltpu.VMEM((NZ, 2, 2, 64, 256), bf),
            pltpu.VMEM((8192, 128), bf),
            pltpu.VMEM((32, 64, 256), bf),
            pltpu.VMEM((32, 64, 256), bf),
            pltpu.VMEM((TP, 8, 128), bf),
            pltpu.VMEM((TP, 8, 128), bf),
            pltpu.VMEM((2, 32, 128), bf),
            pltpu.VMEM((2, 32, 128), bf),
            pltpu.VMEM((32, 8, 128), bf),
            pltpu.VMEM((2, 128, 128), bf),
            pltpu.VMEM((1, 64), jnp.int32),
            pltpu.VMEM((1, 64), jnp.int32),
            pltpu.VMEM((64, 128), jnp.float32),
            pltpu.VMEM((TP * 8, 64), bf),
            pltpu.VMEM((TP * 8, 64), bf),
            pltpu.VMEM((128, 128), jnp.float32),
            pltpu.SMEM((64,), jnp.int32),
            pltpu.SMEM((TP,), jnp.int32),
            dma((9,)),
            dma((2,)),
            dma((2,)),
            dma((64,)),
            dma((64,)),
            dma((31,)),
            dma((31,)),
            dma((32,)),
            dma((32,)),
            dma,
            dma,
            pltpu.SemaphoreType.REGULAR((6,)),
        ],
        compiler_params=pltpu.CompilerParams(
            collective_id=0, has_side_effects=True, vmem_limit_bytes=60 * 1024 * 1024
        ),
        cost_estimate=pl.CostEstimate(
            flops=2 * 128 * 8192 * 128, bytes_accessed=5 * 1024 * 1024, transcendentals=0
        ),
    )(
        hidden_old,
        queries_old,
        kv_weight,
        cache,
        lengths.reshape(1, 64),
        slot.reshape(1, 64),
        slot,
        hidden_new,
        queries_new,
    )
    return attended_old, attended_new, served.reshape(2, 1024, 256)


def solution(mesh):
    placed = (
        P(None, "rep", "tp"),
        P(("rep", "tp"), None, None),
        P(None, "tp"),
        P(("rep", "tp"), None, None),
        P("rep"),
        P("rep"),
        P(None, "rep", "tp"),
        P(("rep", "tp"), None, None),
    )
    return jax.shard_map(
        shards,
        mesh=mesh,
        in_specs=placed,
        out_specs=(
            P(("rep", "tp"), None, None),
            P(("rep", "tp"), None, None),
            P(("rep", "tp"), None, None),
        ),
        check_vma=False,
    )
```

time: 110 us -> 101 us (0.918)
  Pallas kernels: 98.3 us -> 94.7 us
  matrix products: 3.12 us -> 0 us
  other arithmetic: 1.96 us -> 0 us
    pallas_call x1, Pallas kernels: 98.3 us -> 94.7 us  [shards(): pl.pallas_call(step_kernel, out_shape=(jax.ShapeDtypeStruct((32, 8, 128),...]
    dot_general x6 -> x0, matrix products: 3.12 us -> none  [the longest x2 1.9 us: attend(): jnp.einsum('abgl,able->abge', weights, value_rows, preferred_element_type...]
    unnamed x20 -> x3, local copies, waits for them, and re-layouts: 4.53 us -> 5.21 us
where the time goes in v2:
time: 101 us
  Pallas kernels  94.7 us (94%)
  local copies, waits for them, and re-layouts  5.21 us (5%)
    pallas_call x1, Pallas kernels, shards(): pl.pallas_call(step_kernel, out_shape=(jax.ShapeDtypeStruct((32, 8, 128),...  94.7 us
    unnamed x3, local copies, waits for them, and re-layouts  5.21 us

profile of v2, /device:TPU:24, one launch (start us, length us, event | category | flops | bytes accessed | tf_op | source)
XLA Modules:
  0.0 100.6 jit_solution(9039633744414802662)
XLA Ops:
  0.6 94.7 %shard_map.103 = (bf16[32,8,128]{2,1,0:T(8,128)(2,1)}, bf16[2,128,128]{2,1,0:T(8,128)(2,1)}, bf16[2,16,64,256]{3,2,1,0:T(8,128)(2,1)}) custom-call(bf16[2,64,256]{2,1,0:T(8,128)(2,1)} %hold_hbm.1, bf16[32,8,128]{2,1,0:T(8,128)(2,1)} %qold_hbm.1, bf16[8192,128]{1,0:T(8,128)(2,1)} %w_hbm.1, bf16[32,64,256]{2,1,0:T(8,128)(2,1)} %cache_hbm.1, s32[1,64]{1,0:T(1,128)} %bitcast.5, ...), custom_call_target="tpu_custom_call" | custom-call | flops 268435456 | bytes 5242880 | tf_op jit(solution)/shard_map/pallas_call | solution.py:344
  95.4 1.5 %copy.14 = bf16[32,8,128]{2,1,0:T(8,128)(2,1)} copy(bf16[32,8,128]{2,1,0:T(8,128)(2,1)} %get-tuple-element.12) | data formatting | bytes 131072
  96.8 1.5 %copy.15 = bf16[2,128,128]{2,1,0:T(8,128)(2,1)} copy(bf16[2,128,128]{2,1,0:T(8,128)(2,1)} %get-tuple-element.13) | data formatting | bytes 131072
  98.3 2.3 %copy.16 = bf16[2,1024,256]{2,1,0:T(8,128)(2,1)} copy(bf16[2,1024,256]{2,1,0:T(8,128)(2,1)} %bitcast.3) | data formatting | bytes 2097152

commit v3 on v2

--- a/solution.py
+++ b/solution.py
@@ -336,19 +336,32 @@
         c.wait_send()
 
 
+def hand_over(old_in, new_in, served_in, old_ref, new_ref, served_ref, sem):
+    copies = [
+        pltpu.make_async_copy(served_in, served_ref, sem.at[0]),
+        pltpu.make_async_copy(old_in, old_ref, sem.at[1]),
+        pltpu.make_async_copy(new_in, new_ref, sem.at[2]),
+    ]
+    for c in copies:
+        c.start()
+    for c in copies:
+        c.wait()
+
+
 def shards(hidden_old, queries_old, kv_weight, cache, lengths, slot, hidden_new, queries_new):
+    hbm = pl.BlockSpec(memory_space=pltpu.HBM)
     any_spec = pl.BlockSpec(memory_space=pl.ANY)
     vmem = pl.BlockSpec(memory_space=pltpu.VMEM)
     dma = pltpu.SemaphoreType.DMA
     bf = jnp.bfloat16
-    attended_old, attended_new, served = pl.pallas_call(
+    parts = pl.pallas_call(
         step_kernel,
         out_shape=(
             jax.ShapeDtypeStruct((32, 8, 128), bf),
             jax.ShapeDtypeStruct((2, 128, 128), bf),
             jax.ShapeDtypeStruct((2, 16, 64, 256), bf),
         ),
-        in_specs=[any_spec] * 9,
+        in_specs=[hbm] * 9,
         out_specs=(vmem, vmem, vmem),
         scratch_shapes=[
             pltpu.VMEM((NZ, 2, 2, 64, 256), bf),
@@ -383,22 +396,36 @@
             pltpu.SemaphoreType.REGULAR((6,)),
         ],
         compiler_params=pltpu.CompilerParams(
-            collective_id=0, has_side_effects=True, vmem_limit_bytes=60 * 1024 * 1024
+            collective_id=0, has_side_effects=True, vmem_limit_bytes=24 * 1024 * 1024
         ),
         cost_estimate=pl.CostEstimate(
             flops=2 * 128 * 8192 * 128, bytes_accessed=5 * 1024 * 1024, transcendentals=0
         ),
     )(
-        hidden_old,
-        queries_old,
-        kv_weight,
-        cache,
-        lengths.reshape(1, 64),
-        slot.reshape(1, 64),
-        slot,
-        hidden_new,
-        queries_new,
-    )
+        *(
+            pltpu.with_memory_space_constraint(array, pltpu.HBM)
+            for array in (
+                hidden_old,
+                queries_old,
+                kv_weight,
+                cache,
+                lengths.reshape(1, 64),
+                slot.reshape(1, 64),
+                slot,
+                hidden_new,
+                queries_new,
+            )
+        )
+    )
+    attended_old, attended_new, served = pl.pallas_call(
+        hand_over,
+        out_shape=tuple(jax.ShapeDtypeStruct(part.shape, part.dtype) for part in parts),
+        in_specs=[any_spec] * 3,
+        out_specs=(any_spec,) * 3,
+        scratch_shapes=[dma((3,))],
+        compiler_params=pltpu.CompilerParams(vmem_limit_bytes=16 * 1024 * 1024),
+        cost_estimate=pl.CostEstimate(flops=0, bytes_accessed=2400000, transcendentals=0),
+    )(*parts)
     return attended_old, attended_new, served.reshape(2, 1024, 256)
 
 

time: 101 us -> 95.5 us (0.946)
  local copies, waits for them, and re-layouts: 5.21 us -> 0 us
    unnamed x3 -> x0, local copies, waits for them, and re-layouts: 5.21 us -> none
    pallas_call x1, Pallas kernels: 94.7 us -> 93.7 us  [shards(): pl.pallas_call(step_kernel, out_shape=(jax.ShapeDtypeStruct((32, 8, 128),...]
    pallas_call x0 -> x1, Pallas kernels: none -> 1.02 us  [shards(): pl.pallas_call(hand_over, out_shape=tuple((jax.ShapeDtypeStruct(part.shap...]
where the time goes in v3:
time: 95.5 us; the launch traced here: 95.4 us
  Pallas kernels  94.7 us (99%)
    pallas_call x1, Pallas kernels, shards(): pl.pallas_call(step_kernel, out_shape=(jax.ShapeDtypeStruct((32, 8, 128),...  93.7 us

profile of v3, /device:TPU:24, one launch (start us, length us, event | category | flops | bytes accessed | tf_op | source)
XLA Modules:
  0.0 95.4 jit_solution(5039917340598319622)
XLA Ops:
  0.6 93.7 %shard_map.103 = (bf16[32,8,128]{2,1,0:T(8,128)(2,1)S(1)}, bf16[2,128,128]{2,1,0:T(8,128)(2,1)S(1)}, bf16[2,16,64,256]{3,2,1,0:T(8,128)(2,1)S(1)}) custom-call(bf16[2,64,256]{2,1,0:T(8,128)(2,1)} %hold_hbm.1, bf16[32,8,128]{2,1,0:T(8,128)(2,1)} %qold_hbm.1, bf16[8192,128]{1,0:T(8,128)(2,1)} %w_hbm.1, bf16[32,64,256]{2,1,0:T(8,128)(2,1)} %cache_hbm.1, ...), custom_call_target="tpu_custom_call" | custom-call | flops 268435456 | bytes 5242880 | tf_op jit(solution)/shard_map/pallas_call | solution.py:357
  94.3 1.0 %shard_map.104 = (bf16[32,8,128]{2,1,0:T(8,128)(2,1)}, bf16[2,128,128]{2,1,0:T(8,128)(2,1)}, bf16[2,16,64,256]{3,2,1,0:T(8,128)(2,1)}) custom-call(bf16[32,8,128]{2,1,0:T(8,128)(2,1)S(1)} %get-tuple-element.9.old_in, bf16[2,128,128]{2,1,0:T(8,128)(2,1)S(1)} %get-tuple-element.10.new_in, bf16[2,16,64,256]{3,2,1,0:T(8,128)(2,1)S(1)} %get-tuple-element.11.served_in), custom_call_target="tpu_custom_call" | custom-call | bytes 2400000 | tf_op jit(solution)/shard_map/pallas_call | solution.py:420

commit v4 on v3

--- a/solution.py
+++ b/solution.py
@@ -85,6 +85,9 @@
     pick_old,
     pick_new,
     acc,
+    mixed_buf,
+    top_buf,
+    total_buf,
     slot_s,
     order_s,
     local_sem,
@@ -131,17 +134,7 @@
     ]
     for c in loads:
         c.start()
-    loads[0].wait()
-
-    def find(u, carry):
-        found = 0
-        for r in range(32):
-            found = jnp.where(slot_s[32 * half + r] == 2 * u + half, r, found)
-        order_s[u] = found
-        return carry
-
-    lax.fori_loop(0, TP, find, 0)
-    for c in loads[1:5]:
+    for c in loads[1:3]:
         c.wait()
 
     pl.semaphore_wait(barrier, 3)
@@ -184,13 +177,22 @@
         for way in range(2):
             pl.semaphore_wait(near_sem.at[2 * i + way], 1)
 
-    greet(0, 1)
+    loads[0].wait()
+
+    def find(u, carry):
+        found = 0
+        for r in range(32):
+            found = jnp.where(slot_s[32 * half + r] == 2 * u + half, r, found)
+        order_s[u] = found
+        return carry
+
+    lax.fori_loop(0, TP, find, 0)
+    for c in loads[3:5]:
+        c.wait()
     for p in range(2):
         xcopies[p].wait_recv()
         for way in range(2):
             forward(1, way, 0, p)
-    greeted(0)
-    greet(1, 2)
 
     acc[...] = jnp.zeros_like(acc)
     rid = lax.broadcasted_iota(jnp.int32, (TP * 8, 64), 0)
@@ -212,10 +214,7 @@
     column = jnp.sum(jnp.where(eye, lengths_f, 0.0), axis=1, keepdims=True)
     len_cols[...] = jnp.broadcast_to(column, (64, 128))
 
-    greeted(1)
-    greet(2, 4)
     loads[5].wait()
-    greeted(2)
 
     order = [(0, 8)]
     for dz in range(7, 0, -1):
@@ -244,7 +243,6 @@
             hbuf[slot, plane].reshape(128, 256), wbuf[rows, :], preferred_element_type=jnp.float32
         )
 
-    send_blocks(5)
     loads[6].wait()
     for k in range(8):
         for stream in range(2):
@@ -255,7 +253,14 @@
                     ring(stream, way, k, p).wait_recv()
                     if k + 1 < steps[stream][way]:
                         forward(stream, way, k + 1, p)
-        send_blocks(4)
+        if k == 0:
+            greet(0, 2)
+        elif k == 1:
+            greeted(0)
+            greet(1, 4)
+        elif k == 2:
+            greeted(1)
+        send_blocks((0, 0, 5, 3, 3, 3, 3, 3)[k])
         if k == 0:
             multiply(0, z)
             multiply(1, z)
@@ -279,6 +284,7 @@
         c = remote(mbuf.at[target], fbuf.at[me], ms_sem.at[i], mr_sem.at[i], target)
         c.start()
         message_copies.append(c)
+    send_blocks(31)
     pbuf[half] = obuf[half]
     fbuf[me] = mbuf[me]
     served_ref[half, head] = cbuf[order_s[me]]
@@ -301,35 +307,59 @@
         ]
         old_ref[entries] = with_tokens(qobuf[entries], stored_old[c], tokens).astype(jnp.bfloat16)
 
-    for c in cache_copies:
-        c.wait()
-    stored_new = []
     new_len = []
     for p in range(2):
         count = jnp.sum(
             jnp.where(slot_row[...] == 2 * me + p, lengths_f, 0.0), axis=1, keepdims=True
         )
-        new_len.append(count)
-        queries = qnbuf[p].reshape(16, 8, 128)
-        stored_new.append(stored_part(queries, served_ref[p], count.reshape(1, 1, 1)))
+        new_len.append(count.reshape(1, 1, 1))
+
+    def arrived(group):
+        places = []
+        for i in group:
+            if i < len(order):
+                cache_copies[i].wait_recv()
+                dx, dz = order[i]
+                zs = (z + NZ - dz) % NZ
+                places.append((zs % 2, ((x + dx) % 2 * NZ + zs) // 2))
+            else:
+                places.append((half, head))
+        queries = jnp.stack(
+            [qnbuf[h, a] for h, a in places]
+        )
+        blocks = jnp.stack([served_ref[h, a] for h, a in places])
+        limit = jnp.concatenate(
+            [jnp.where(h == 0, new_len[0], new_len[1]) for h, _ in places], axis=0
+        )
+        mixed, top, total = stored_part(queries, blocks, limit)
+        for n, (h, a) in enumerate(places):
+            mixed_buf[h, a] = mixed[n]
+            top_buf[h, a] = jnp.broadcast_to(top[n], (8, 128))
+            total_buf[h, a] = jnp.broadcast_to(total[n], (8, 128))
+
+    for g in range(4):
+        arrived(range(8 * g, 8 * g + 8))
     for c in message_copies:
         c.wait()
     received = fbuf[...].astype(jnp.float32).reshape(16, 2, 8, 128)
     for p in range(2):
-        queries = qnbuf[p].reshape(16, 8, 128)
+        queries = qnbuf[p]
         first_key, first_value = received[:, 0, p : p + 1], received[:, 1, p : p + 1]
         tokens = [
             (first_key, first_value),
             (received[:, 0, p + 2 : p + 3], received[:, 1, p + 2 : p + 3]),
         ]
-        attended = with_tokens(queries, stored_new[p], tokens)
+        stored = (mixed_buf[p], top_buf[p][:, :, :1], total_buf[p][:, :, :1])
+        attended = with_tokens(queries, stored, tokens)
         new_ref[p] = attended.astype(jnp.bfloat16).reshape(128, 128)
         row = lax.broadcasted_iota(jnp.int32, (1, 64, 256), 1).astype(jnp.float32)
         token = jnp.concatenate([first_key, first_value], axis=2)
         served_ref[p] = jnp.where(
-            row == new_len[p].reshape(1, 1, 1), token, served_ref[p].astype(jnp.float32)
+            row == new_len[p], token, served_ref[p].astype(jnp.float32)
         ).astype(jnp.bfloat16)
 
+    for c in cache_copies:
+        c.wait_send()
     for c in sent:
         c.wait_send()
     for c in xcopies:
@@ -373,13 +403,16 @@
             pltpu.VMEM((2, 32, 128), bf),
             pltpu.VMEM((2, 32, 128), bf),
             pltpu.VMEM((32, 8, 128), bf),
-            pltpu.VMEM((2, 128, 128), bf),
+            pltpu.VMEM((2, 16, 8, 128), bf),
             pltpu.VMEM((1, 64), jnp.int32),
             pltpu.VMEM((1, 64), jnp.int32),
             pltpu.VMEM((64, 128), jnp.float32),
             pltpu.VMEM((TP * 8, 64), bf),
             pltpu.VMEM((TP * 8, 64), bf),
             pltpu.VMEM((128, 128), jnp.float32),
+            pltpu.VMEM((2, 16, 8, 128), jnp.float32),
+            pltpu.VMEM((2, 16, 8, 128), jnp.float32),
+            pltpu.VMEM((2, 16, 8, 128), jnp.float32),
             pltpu.SMEM((64,), jnp.int32),
             pltpu.SMEM((TP,), jnp.int32),
             dma((9,)),
@@ -393,7 +426,7 @@
             dma((32,)),
             dma,
             dma,
-            pltpu.SemaphoreType.REGULAR((6,)),
+            pltpu.SemaphoreType.REGULAR((4,)),
         ],
         compiler_params=pltpu.CompilerParams(
             collective_id=0, has_side_effects=True, vmem_limit_bytes=24 * 1024 * 1024
@@ -413,7 +446,7 @@
                 slot.reshape(1, 64),
                 slot,
                 hidden_new,
-                queries_new,
+                queries_new.reshape(2, 16, 8, 128),
             )
         )
     )

time: 95.5 us -> 92.4 us (0.968)
  Pallas kernels: 94.7 us -> 91.7 us
    pallas_call x1, Pallas kernels: 93.7 us -> 90.6 us  [shards(): pl.pallas_call(step_kernel, out_shape=(jax.ShapeDtypeStruct((32, 8, 128),...]
where the time goes in v4:
time: 92.4 us; the launch traced here: 92.3 us
  Pallas kernels  91.7 us (99%)
    pallas_call x1, Pallas kernels, shards(): pl.pallas_call(step_kernel, out_shape=(jax.ShapeDtypeStruct((32, 8, 128),...  90.6 us

profile of v4, /device:TPU:24, one launch (start us, length us, event | category | flops | bytes accessed | tf_op | source)
XLA Modules:
  0.0 92.3 jit_solution(17945675347224333549)
XLA Ops:
  0.6 90.6 %shard_map.103 = (bf16[32,8,128]{2,1,0:T(8,128)(2,1)S(1)}, bf16[2,128,128]{2,1,0:T(8,128)(2,1)S(1)}, bf16[2,16,64,256]{3,2,1,0:T(8,128)(2,1)S(1)}) custom-call(bf16[2,64,256]{2,1,0:T(8,128)(2,1)} %hold_hbm.1, bf16[32,8,128]{2,1,0:T(8,128)(2,1)} %qold_hbm.1, bf16[8192,128]{1,0:T(8,128)(2,1)} %w_hbm.1, bf16[32,64,256]{2,1,0:T(8,128)(2,1)} %cache_hbm.1, ...), custom_call_target="tpu_custom_call" | custom-call | flops 268435456 | bytes 5242880 | tf_op jit(solution)/shard_map/pallas_call | solution.py:387
  91.3 1.0 %shard_map.104 = (bf16[32,8,128]{2,1,0:T(8,128)(2,1)}, bf16[2,128,128]{2,1,0:T(8,128)(2,1)}, bf16[2,16,64,256]{3,2,1,0:T(8,128)(2,1)}) custom-call(bf16[32,8,128]{2,1,0:T(8,128)(2,1)S(1)} %get-tuple-element.9.old_in, bf16[2,128,128]{2,1,0:T(8,128)(2,1)S(1)} %get-tuple-element.10.new_in, bf16[2,16,64,256]{3,2,1,0:T(8,128)(2,1)S(1)} %get-tuple-element.11.served_in), custom_call_target="tpu_custom_call" | custom-call | bytes 2400000 | tf_op jit(solution)/shard_map/pallas_call | solution.py:453

commit v5 on v4

--- a/solution.py
+++ b/solution.py
@@ -101,6 +101,8 @@
     mr_sem,
     ps_sem,
     pr_sem,
+    ys_sem,
+    yr_sem,
     near_sem,
 ):
     me = lax.axis_index("tp")
@@ -195,18 +197,15 @@
             forward(1, way, 0, p)
 
     acc[...] = jnp.zeros_like(acc)
-    rid = lax.broadcasted_iota(jnp.int32, (TP * 8, 64), 0)
-    col = lax.broadcasted_iota(jnp.int32, (TP * 8, 64), 1)
-    j = rid & 7
-    d = rid >> 3
+    rid = lax.broadcasted_iota(jnp.int32, (NZ * 8, 64), 0)
+    col = lax.broadcasted_iota(jnp.int32, (NZ * 8, 64), 1)
+    j = rid & 3
+    plane = jnp.where((rid & 7) < 4, x, other)
+    row = 2 * (plane * NZ + (rid >> 3)) + (j & 1)
     pick_old[...] = (
-        (slot_row[...] == jnp.where(j < 2, 2 * d + j, -1)).astype(jnp.float32).astype(jnp.bfloat16)
-    )
-    pick_new[...] = (
-        (col == jnp.where((j >= 2) & (j < 4), 2 * d + j - 2, -1))
-        .astype(jnp.float32)
-        .astype(jnp.bfloat16)
-    )
+        (slot_row[...] == jnp.where(j < 2, row, -1)).astype(jnp.float32).astype(jnp.bfloat16)
+    )
+    pick_new[...] = (col == jnp.where(j < 2, -1, row)).astype(jnp.float32).astype(jnp.bfloat16)
     eye = lax.broadcasted_iota(jnp.int32, (64, 64), 0) == lax.broadcasted_iota(
         jnp.int32, (64, 64), 1
     )
@@ -277,16 +276,17 @@
     messages = jnp.dot(pick_old[...], fresh[:64], preferred_element_type=jnp.float32) + jnp.dot(
         pick_new[...], fresh[64:], preferred_element_type=jnp.float32
     )
-    mbuf[...] = messages.astype(jnp.bfloat16).reshape(TP, 8, 128)
+    mbuf[...] = messages.astype(jnp.bfloat16).reshape(NZ, 8, 128)
     message_copies = []
-    for i in range(1, TP):
-        target = (me + i) % TP
-        c = remote(mbuf.at[target], fbuf.at[me], ms_sem.at[i], mr_sem.at[i], target)
+    for i, dz in enumerate((8, 7, 9, 6, 10, 5, 11, 4, 12, 3, 13, 2, 14, 1, 15)):
+        c = remote(
+            mbuf.at[(z + dz) % NZ], fbuf.at[me], ms_sem.at[i], mr_sem.at[i], on_ring(dz)
+        )
         c.start()
         message_copies.append(c)
     send_blocks(31)
     pbuf[half] = obuf[half]
-    fbuf[me] = mbuf[me]
+    fbuf[me] = mbuf[z]
     served_ref[half, head] = cbuf[order_s[me]]
 
     loads[7].wait()
@@ -307,6 +307,11 @@
         ]
         old_ref[entries] = with_tokens(qobuf[entries], stored_old[c], tokens).astype(jnp.bfloat16)
 
+    for c in message_copies:
+        c.wait()
+    ring_rows = fbuf.at[pl.ds(pl.multiple_of(x * NZ, NZ), NZ)]
+    relay = remote(ring_rows, ring_rows, ys_sem, yr_sem, twin)
+    relay.start()
     new_len = []
     for p in range(2):
         count = jnp.sum(
@@ -339,16 +344,17 @@
 
     for g in range(4):
         arrived(range(8 * g, 8 * g + 8))
-    for c in message_copies:
-        c.wait()
+    relay.wait()
     received = fbuf[...].astype(jnp.float32).reshape(16, 2, 8, 128)
+    mine = (lax.broadcasted_iota(jnp.int32, (16, 1, 128), 0) >> 3) == x
+
+    def token_row(kind, j):
+        return jnp.where(mine, received[:, kind, j : j + 1], received[:, kind, j + 4 : j + 5])
+
     for p in range(2):
         queries = qnbuf[p]
-        first_key, first_value = received[:, 0, p : p + 1], received[:, 1, p : p + 1]
-        tokens = [
-            (first_key, first_value),
-            (received[:, 0, p + 2 : p + 3], received[:, 1, p + 2 : p + 3]),
-        ]
+        first_key, first_value = token_row(0, p), token_row(1, p)
+        tokens = [(first_key, first_value), (token_row(0, p + 2), token_row(1, p + 2))]
         stored = (mixed_buf[p], top_buf[p][:, :, :1], total_buf[p][:, :, :1])
         attended = with_tokens(queries, stored, tokens)
         new_ref[p] = attended.astype(jnp.bfloat16).reshape(128, 128)
@@ -398,7 +404,7 @@
             pltpu.VMEM((8192, 128), bf),
             pltpu.VMEM((32, 64, 256), bf),
             pltpu.VMEM((32, 64, 256), bf),
-            pltpu.VMEM((TP, 8, 128), bf),
+            pltpu.VMEM((NZ, 8, 128), bf),
             pltpu.VMEM((TP, 8, 128), bf),
             pltpu.VMEM((2, 32, 128), bf),
             pltpu.VMEM((2, 32, 128), bf),
@@ -407,8 +413,8 @@
             pltpu.VMEM((1, 64), jnp.int32),
             pltpu.VMEM((1, 64), jnp.int32),
             pltpu.VMEM((64, 128), jnp.float32),
-            pltpu.VMEM((TP * 8, 64), bf),
-            pltpu.VMEM((TP * 8, 64), bf),
+            pltpu.VMEM((NZ * 8, 64), bf),
+            pltpu.VMEM((NZ * 8, 64), bf),
             pltpu.VMEM((128, 128), jnp.float32),
             pltpu.VMEM((2, 16, 8, 128), jnp.float32),
             pltpu.VMEM((2, 16, 8, 128), jnp.float32),
@@ -422,8 +428,10 @@
             dma((64,)),
             dma((31,)),
             dma((31,)),
-            dma((32,)),
-            dma((32,)),
+            dma((15,)),
+            dma((15,)),
+            dma,
+            dma,
             dma,
             dma,
             pltpu.SemaphoreType.REGULAR((4,)),

time: 92.4 us -> 90.6 us (0.981)
  Pallas kernels: 91.7 us -> 89.9 us
    pallas_call x1, Pallas kernels: 90.6 us -> 88.9 us  [shards(): pl.pallas_call(step_kernel, out_shape=(jax.ShapeDtypeStruct((32, 8, 128),...]
where the time goes in v5:
time: 90.6 us; the launch traced here: 90.5 us
  Pallas kernels  89.9 us (99%)
    pallas_call x1, Pallas kernels, shards(): pl.pallas_call(step_kernel, out_shape=(jax.ShapeDtypeStruct((32, 8, 128),...  88.9 us

profile of v5, /device:TPU:24, one launch (start us, length us, event | category | flops | bytes accessed | tf_op | source)
XLA Modules:
  0.0 90.5 jit_solution(14127274712150817818)
XLA Ops:
  0.6 88.9 %shard_map.103 = (bf16[32,8,128]{2,1,0:T(8,128)(2,1)S(1)}, bf16[2,128,128]{2,1,0:T(8,128)(2,1)S(1)}, bf16[2,16,64,256]{3,2,1,0:T(8,128)(2,1)S(1)}) custom-call(bf16[2,64,256]{2,1,0:T(8,128)(2,1)} %hold_hbm.1, bf16[32,8,128]{2,1,0:T(8,128)(2,1)} %qold_hbm.1, bf16[8192,128]{1,0:T(8,128)(2,1)} %w_hbm.1, bf16[32,64,256]{2,1,0:T(8,128)(2,1)} %cache_hbm.1, ...), custom_call_target="tpu_custom_call" | custom-call | flops 268435456 | bytes 5242880 | tf_op jit(solution)/shard_map/pallas_call | solution.py:393
  89.5 1.0 %shard_map.104 = (bf16[32,8,128]{2,1,0:T(8,128)(2,1)}, bf16[2,128,128]{2,1,0:T(8,128)(2,1)}, bf16[2,16,64,256]{3,2,1,0:T(8,128)(2,1)}) custom-call(bf16[32,8,128]{2,1,0:T(8,128)(2,1)S(1)} %get-tuple-element.9.old_in, bf16[2,128,128]{2,1,0:T(8,128)(2,1)S(1)} %get-tuple-element.10.new_in, bf16[2,16,64,256]{3,2,1,0:T(8,128)(2,1)S(1)} %get-tuple-element.11.served_in), custom_call_target="tpu_custom_call" | custom-call | bytes 2400000 | tf_op jit(solution)/shard_map/pallas_call | solution.py:461

commit v6 on v5

--- a/solution.py
+++ b/solution.py
@@ -259,7 +259,7 @@
             greet(1, 4)
         elif k == 2:
             greeted(1)
-        send_blocks((0, 0, 5, 3, 3, 3, 3, 3)[k])
+        send_blocks((0, 0, 6, 4, 4, 3, 2, 1)[k])
         if k == 0:
             multiply(0, z)
             multiply(1, z)

time: 90.6 us -> 91.9 us (1.014); the launches traced: 90.5 us -> 90.4 us
  no operation moved by 1% of the time
where the time goes in v6:
time: 91.9 us; the launch traced here: 90.4 us
  Pallas kernels  89.7 us (98%)
    pallas_call x1, Pallas kernels, shards(): pl.pallas_call(step_kernel, out_shape=(jax.ShapeDtypeStruct((32, 8, 128),...  88.7 us

profile of v6, /device:TPU:24, one launch (start us, length us, event | category | flops | bytes accessed | tf_op | source)
XLA Modules:
  0.0 90.4 jit_solution(17461095244646387820)
XLA Ops:
  0.6 88.7 %shard_map.103 = (bf16[32,8,128]{2,1,0:T(8,128)(2,1)S(1)}, bf16[2,128,128]{2,1,0:T(8,128)(2,1)S(1)}, bf16[2,16,64,256]{3,2,1,0:T(8,128)(2,1)S(1)}) custom-call(bf16[2,64,256]{2,1,0:T(8,128)(2,1)} %hold_hbm.1, bf16[32,8,128]{2,1,0:T(8,128)(2,1)} %qold_hbm.1, bf16[8192,128]{1,0:T(8,128)(2,1)} %w_hbm.1, bf16[32,64,256]{2,1,0:T(8,128)(2,1)} %cache_hbm.1, ...), custom_call_target="tpu_custom_call" | custom-call | flops 268435456 | bytes 5242880 | tf_op jit(solution)/shard_map/pallas_call | solution.py:393
  89.4 1.0 %shard_map.104 = (bf16[32,8,128]{2,1,0:T(8,128)(2,1)}, bf16[2,128,128]{2,1,0:T(8,128)(2,1)}, bf16[2,16,64,256]{3,2,1,0:T(8,128)(2,1)}) custom-call(bf16[32,8,128]{2,1,0:T(8,128)(2,1)S(1)} %get-tuple-element.9.old_in, bf16[2,128,128]{2,1,0:T(8,128)(2,1)S(1)} %get-tuple-element.10.new_in, bf16[2,16,64,256]{3,2,1,0:T(8,128)(2,1)S(1)} %get-tuple-element.11.served_in), custom_call_target="tpu_custom_call" | custom-call | bytes 2400000 | tf_op jit(solution)/shard_map/pallas_call | solution.py:461
